TPU v7x, 256 devices: a whole 4x4x8 slice. The times are simulated.
256 devices in a mesh: dp: 32 (over x, z_hi, core), comp: 8 (over y, z_lo).
Axes of the slice: x: 4, y: 4, z: 8 (z_hi: 4, z_lo: 2; z = z_hi * 2 + z_lo), core: 2. Of those that a mesh axis runs over, the one named last changes fastest.
Arguments:
- points: bfloat16 [131072, 128], P('dp'), may hold values from -13 to 13
- means: bfloat16 [16384, 128], P(('dp', 'comp')), may hold values from -0.59375 to 0.59375
- variances: float32 [16384], P(('dp', 'comp')), may hold values from 0.5 to 2
- log_weights: float32 [16384], P(('dp', 'comp')), may hold values from -11.5 to -8
Outputs:
- new_means: bfloat16 [16384, 128], P(('dp', 'comp'))
- new_variances: float32 [16384], P(('dp', 'comp'))
- new_log_weights: float32 [16384], P(('dp', 'comp'))
- point_loglik: float32 [131072], P('dp')
All inputs are finite; a program needn't handle non-finite values.
Results may differ from a plain program's by a relative error of at most 0.0023.
Values may be sent and summed in bfloat16 or wider, within the bound.
A program may use at most 64 MiB of HBM per device.

v0:
```python
import math

import jax
import jax.numpy as jnp
from jax import lax
from jax.sharding import PartitionSpec as P

K = 16384


two_pi = 6.283185307179586
prior_strength = 1.0


def log_density(block, block_sq, centres, centre_sq, half_inverse, offset):
    cross = lax.dot_general(
        block, centres, (((1,), (1,)), ((), ())), preferred_element_type=jnp.float32
    )
    return (
        offset[None, :]
        - (block_sq[:, None] + centre_sq[None, :] - 2.0 * cross) * half_inverse[None, :]
    )


def update_step(sums, counts, squares, prior_means, prior_var, total_points, components):
    width = sums.shape[1]
    denom = counts + prior_strength
    centre = (sums + prior_strength * prior_means) / denom[:, None]
    spread = (
        squares
        - 2.0 * jnp.sum(centre * sums, axis=1)
        + counts * jnp.sum(centre * centre, axis=1)
        + prior_strength * width * prior_var
    ) / (width * denom)
    weight = jnp.log((counts + prior_strength) / (total_points + components * prior_strength))
    return (centre.astype(jnp.bfloat16), spread, weight)


def per_device(points, means, variances, log_weights):
    centres = lax.all_gather(means, "dp", axis=0, tiled=True)
    var_group, logw_group = (
        lax.all_gather(variances, "dp", axis=0, tiled=True),
        lax.all_gather(log_weights, "dp", axis=0, tiled=True),
    )
    width = centres.shape[1]
    local_comps = centres.shape[0]
    centre_f = centres.astype(jnp.float32)
    centre_sq = jnp.sum(centre_f * centre_f, axis=1)
    half_inverse = 0.5 / var_group
    offset = logw_group - 0.5 * width * jnp.log(two_pi * var_group)
    npoints = points.shape[0]
    block_rows = math.gcd(npoints, 512)
    block_count = npoints // block_rows
    blocks = points.reshape(block_count, block_rows, width)
    block_sq = jnp.sum(blocks.astype(jnp.float32) ** 2, axis=2)

    def first_pass(item):
        block, bsq = item
        logd = log_density(block, bsq, centres, centre_sq, half_inverse, offset)
        local_peak = jnp.max(logd, axis=1)
        return (local_peak, jnp.sum(jnp.exp(logd - local_peak[:, None]), axis=1))

    local_peak, local_mass = lax.map(first_pass, (blocks, block_sq))
    local_peak = local_peak.reshape(npoints)
    local_mass = local_mass.reshape(npoints)
    row_peak = lax.pmax(local_peak, "comp")
    row_mass = lax.psum(local_mass * jnp.exp(local_peak - row_peak), "comp")
    loglik = row_peak + jnp.log(row_mass)

    def second_pass(carry, item):
        sums, counts, squares = carry
        block, bsq, block_lik = item
        logd = log_density(block, bsq, centres, centre_sq, half_inverse, offset)
        prob = jnp.exp(logd - block_lik[:, None])
        counts = counts + jnp.sum(prob, axis=0)
        squares = squares + jnp.dot(bsq, prob, precision=lax.Precision.HIGHEST)
        sums = sums + lax.dot_general(
            prob,
            block.astype(jnp.float32),
            (((0,), (0,)), ((), ())),
            precision=lax.Precision.HIGHEST,
            preferred_element_type=jnp.float32,
        )
        return ((sums, counts, squares), 0)

    start = (
        jnp.zeros((local_comps, width), jnp.float32),
        jnp.zeros((local_comps,), jnp.float32),
        jnp.zeros((local_comps,), jnp.float32),
    )
    (sums, counts, squares), unused = lax.scan(
        second_pass, start, (blocks, block_sq, loglik.reshape(block_count, block_rows))
    )
    total_points = npoints * lax.axis_size("dp")
    sums, counts, squares = lax.psum((sums, counts, squares), "dp")
    all_means, all_var, all_logw = update_step(
        sums, counts, squares, centre_f, var_group, total_points, K
    )
    owned_rows = means.shape[0]
    first_row = lax.axis_index("dp") * owned_rows
    new_means = lax.dynamic_slice_in_dim(all_means, first_row, owned_rows, 0)
    new_var = lax.dynamic_slice_in_dim(all_var, first_row, owned_rows, 0)
    new_logw = lax.dynamic_slice_in_dim(all_logw, first_row, owned_rows, 0)
    return (new_means, new_var, new_logw, loglik)


def solution(mesh):
    in_specs = (P("dp", None), P(("dp", "comp"), None), P(("dp", "comp")), P(("dp", "comp")))
    out_specs = (P(("dp", "comp"), None), P(("dp", "comp")), P(("dp", "comp")), P("dp"))
    return jax.shard_map(
        per_device, mesh=mesh, in_specs=in_specs, out_specs=out_specs, check_vma=False
    )
```

profile of v0, /device:TPU:1, one launch (start us, length us, event | category | flops | bytes accessed | tf_op | source)
XLA Modules:
  0.0 678.5 jit_solution(8708804405963415788)
XLA Ops:
  7.3 50.4 %all_gather.11 = bf16[2048,128]{1,0:T(8,128)(2,1)S(1)} all-gather(bf16[64,128]{1,0:T(8,128)(2,1)} %param.9), channel_id=1, replica_groups=mesh['dp'=32,'comp'=8] {'dp'}, dimensions={0}, use_global_device_ids=true | all-gather | bytes 540672 | tf_op jit(solution)/shard_map/all_gather | solution.py:40
  63.5 132.1 %all-reduce.3 = (f32[2048]{0:T(1024)S(1)}, f32[2048]{0:T(1024)S(1)}) all-reduce(f32[2048]{0:T(1024)S(1)} %dynamic-update-slice, f32[2048]{0:T(1024)S(1)} %dynamic-update-slice.1), channel_id=1, replica_groups=mesh['dp'=32,'comp'=8] {'dp'}, use_global_device_ids=true, to_apply=%add | all-reduce | flops 4096 | bytes 32768
  195.6 23.3 %while.27 = (s32[]{:T(128)}, f32[8,512]{1,0:T(8,128)S(1)}, f32[8,512]{1,0:T(8,128)S(1)}, f32[2048]{0:T(1024)S(1)}, f32[8,512]{1,0:T(8,128)S(1)}, /*index=5*/f32[...) while((s32[]{:T(128)}, f32[8,512]{1,0:T(8,128)S(1)}, ...), condition=%wide.region_5.6_spmd, body=%wide.region_2.5_spmd.sunk | while | flops 276823040 | bytes 9089657 | solution.py:63
  195.7 2.0 fusion.33
  198.6 2.0 fusion.33
  201.5 2.0 fusion.33
  204.4 2.0 fusion.33
  207.3 2.0 fusion.33
  210.2 2.0 fusion.33
  213.1 2.0 fusion.33
  216.1 2.0 fusion.33
  219.0 27.1 %pmax.7 = f32[4096]{0:T(1024)S(1)} all-reduce(f32[4096]{0:T(1024)S(1)} %bitcast.64), channel_id=1, replica_groups=mesh['dp'=32,'comp'=8] {'comp'}, use_global_device_ids=true, to_apply=%region_6.7 | all-reduce | flops 4096 | bytes 32768 | tf_op jit(solution)/shard_map/pmax | solution.py:66
  246.1 24.2 %psum.28 = f32[4096]{0:T(1024)S(1)} all-reduce(f32[4096]{0:T(1024)S(1)} %exponential_multiply_fusion), channel_id=1, replica_groups=mesh['dp'=32,'comp'=8] {'comp'}, use_global_device_ids=true, to_apply=%region_7.8 | all-reduce | flops 4096 | bytes 32768 | tf_op jit(solution)/shard_map/psum | solution.py:67
  270.8 99.9 %while.28 = (s32[]{:T(128)}, f32[2048,128]{1,0:T(8,128)S(1)}, f32[2048]{0:T(1024)S(1)}, f32[2048]{0:T(1024)S(1)}, f32[2048]{0:T(1024)S(1)}, /*index=5*/f32[8,512...) while((s32[]{:T(128)}, f32[2048,128]{1,0:T(8,128)S(1)}, ...), condition=%wide.region_10.11_spmd.clone, body=%wide.region_8.10_spmd.clone.sunk | while | flops 1899501568 | bytes 32349352 | solution.py:91
  270.9 2.4 fusion.39
  273.2 1.9 copy-done
  275.2 2.1 fusion.40
  277.2 6.0 convolution_add_fusion.2
  283.3 2.4 fusion.39
  287.7 2.1 fusion.40
  289.7 6.0 convolution_add_fusion.2
  295.8 2.4 fusion.39
  298.2 1.9 copy-done
  300.1 2.1 fusion.40
  302.2 6.0 convolution_add_fusion.2
  308.3 2.4 fusion.39
  310.7 1.9 copy-done
  312.6 2.1 fusion.40
  314.7 6.0 convolution_add_fusion.2
  320.8 2.4 fusion.39
  323.2 1.9 copy-done
  325.1 2.1 fusion.40
  327.2 6.0 convolution_add_fusion.2
  333.3 2.4 fusion.39
  335.7 1.9 copy-done
  337.6 2.1 fusion.40
  339.7 6.0 convolution_add_fusion.2
  345.8 2.4 fusion.39
  348.2 1.9 copy-done
  350.1 2.1 fusion.40
  352.2 6.0 convolution_add_fusion.2
  358.3 2.4 fusion.39
  360.7 1.9 copy-done
  362.6 2.1 fusion.40
  364.7 6.0 convolution_add_fusion.2
  371.8 152.5 %all-reduce.2 = (f32[2048]{0:T(1024)S(1)}, f32[2048]{0:T(1024)S(1)}) all-reduce(f32[2048]{0:T(1024)S(1)} %get-tuple-element.114, f32[2048]{0:T(1024)S(1)} %get-tuple-element.115), channel_id=1, replica_groups=mesh['dp'=32,'comp'=8] {'dp'}, use_global_device_ids=true, to_apply=%region_12.13 | all-reduce | flops 4096 | bytes 32768 | tf_op jit(solution)/shard_map/psum | solution.py:95
  524.3 144.1 %all-reduce.6.cloned.1.call-done = f32[2048,128]{1,0:T(8,128)} async-done(((f32[2048,128]{1,0:T(8,128)}), f32[2048,128]{1,0:T(8,128)}) %all-reduce.6.cloned.1.call-update) | async-done | bytes 1048592 | tf_op jit(solution)/shard_map/psum | solution.py:95
  668.4 2.1 multiply_reduce_fusion.2
  (93 shorter events, 17.0 us)
Async XLA Ops:
  7.2 661.2 %all-reduce.6.cloned.1.call-start = ((), (), s32[]{:S(2)}) async-start(), calls=%async_computation | async-start | bytes 2097152 | tf_op jit(solution)/shard_map/psum | solution.py:95
  270.2 0.6 copy-start.2
  273.2 1.9 copy-start
  285.7 1.9 copy-start
  298.2 1.9 copy-start
  310.7 1.9 copy-start
  323.2 1.9 copy-start
  335.7 1.9 copy-start
  348.2 1.9 copy-start
  360.7 1.9 copy-start
  370.7 1.0 copy-start.1
Sparse Core Ops, SparseCore 0:
  371.9 296.4 all-reduce.5
where the time goes:
time: 679 us
  blocking collectives  386 us (57%)
  waiting for transfers between devices  144 us (21%)
  matrix products  100 us (15%)
  local copies, waits for them, and re-layouts  21.7 us (3%)
  between operations  14.8 us (2%)
  other arithmetic  10.7 us (2%)
    psum x1, blocking collectives, per_device(): sums, counts, squares = lax.psum((sums, counts, squares), 'dp')  152 us
    psum x1, waiting for transfers between devices, per_device(): sums, counts, squares = lax.psum((sums, counts, squares), 'dp')  144 us
    unnamed x1, blocking collectives  132 us
    all_gather x1, blocking collectives, per_device(): centres = lax.all_gather(means, 'dp', axis=0, tiled=True)  50.4 us
    dot_general x8, matrix products, second_pass(): lax.dot_general(prob, block.astype(jnp.float32), (((0,), (0,)), ((), ()))...  48.3 us
    dot_general x16, matrix products, log_density(): lax.dot_general(block, centres, (((1,), (1,)), ((), ())), preferred_eleme...  35.3 us
    pmax x1, blocking collectives, per_device(): row_peak = lax.pmax(local_peak, 'comp')  27.1 us
    psum x1, blocking collectives, per_device(): row_mass = lax.psum(local_mass * jnp.exp(local_peak - row_peak), 'comp')  24.2 us
  transfers between devices with their start and end apart: 1, of which 1 were waited for; matrix products, arithmetic and copies ran while one was open for 0% of the time, Pallas kernels for 0%

commit v1 on v0

v1 whole, which is shorter than its diff:
```python
import functools

import jax
import jax.numpy as jnp
from jax import lax
from jax.experimental import pallas as pl
from jax.experimental.pallas import tpu as pltpu
from jax.sharding import PartitionSpec as P

MESH = pl.DeviceIdType.MESH
F32 = jnp.float32
BF16 = jnp.bfloat16

COMPONENTS = 16384
LOG2E = 1.4426950408889634
LN2 = 0.6931471805599453
TWO_PI = 6.283185307179586

XS, ZS, CORES = 4, 4, 2
WIDTH = 128
OWN = 64
BLOCK = 80
CHUNK = 512
TILE = 512

BASE = {
    (0, 0): 0, (1, 0): 4,
    (0, 1): 8, (0, 3): 12,
    (1, 1): 16, (1, 3): 20,
    (0, 2): 24, (1, 2): 28,
}
SIB = {0: 0, 1: 4, 3: 8, 2: 12}


def split3(v):
    hi = v.astype(BF16).astype(F32)
    mid = (v - hi).astype(BF16).astype(F32)
    lo = (v - hi - mid).astype(BF16).astype(F32)
    return hi, mid, lo


def rows16(parts, lanes):
    row = lax.broadcasted_iota(jnp.int32, (16, lanes), 0)
    out = jnp.zeros((16, lanes), F32)
    for i, part in parts.items():
        out = jnp.where(row == i, jnp.broadcast_to(part, (16, lanes)), out)
    return out


def spread_rows(tile, table):
    return lax.dot_general(tile, table, (((0,), (0,)), ((), ())), preferred_element_type=F32)


def body(
    comps, npoints, total_points,
    points, means, var, logw,
    out_means, out_var, out_logw, out_lik,
    blocks, centres, scale, pts_t, pts, prob, peak, mass, lse, sums, sib,
    x_out, x_in, z_out, z_in,
    g_send, g_recv, l_send, l_recv, r_send, r_recv,
):
    dp = lax.axis_index("dp")
    cp = lax.axis_index("comp")
    core = dp % CORES
    zh = (dp // CORES) % ZS
    xx = dp // (CORES * ZS)

    def dp_at(dx, dz, dc):
        return (
            ((xx + dx) % XS) * (ZS * CORES)
            + ((zh + dz) % ZS) * CORES
            + (core + dc) % CORES
        )

    z_peer = {d: {"dp": dp_at(0, d, 0)} for d in (1, 2, 3)}
    x_peer = {d: {"dp": dp_at(d, 0, 0)} for d in (1, 2, 3)}
    sibling = {"dp": dp_at(0, 0, 1)}
    c_peer = {d: {"comp": (cp + d) % comps} for d in range(1, comps)}

    barrier = pltpu.get_barrier_semaphore()
    everyone = [*z_peer.values(), *x_peer.values(), sibling, *c_peer.values()]
    for peer in everyone:
        pl.semaphore_signal(barrier, inc=1, device_id=peer, device_id_type=MESH)

    m = means[...]
    mf = m.astype(F32)
    msq = mf * mf
    msq_hi = msq.astype(BF16)
    msq_lo = (msq - msq_hi.astype(F32)).astype(BF16)
    ones = jnp.ones((16, WIDTH), BF16)
    nt = (((1,), (1,)), ((), ()))
    centre_sq = (
        lax.dot_general(ones, msq_hi, nt, preferred_element_type=F32)
        + lax.dot_general(ones, msq_lo, nt, preferred_element_type=F32)
    )[0:1, :]
    v = var[...]
    offset = logw[...] - 0.5 * WIDTH * jnp.log(TWO_PI * v)
    e_hi, e_mid, e_lo = split3(v * offset - 0.5 * centre_sq)
    a_hi, a_mid, a_lo = split3(LOG2E / v)
    blocks[0, 0:OWN, :] = m
    blocks[0, OWN:BLOCK, :] = jnp.zeros((16, WIDTH), BF16)
    blocks[0, OWN:BLOCK, 0:OWN] = rows16(
        {0: e_hi, 1: e_mid, 2: e_lo, 3: a_hi, 4: a_mid, 5: a_lo, 6: jnp.ones_like(v)}, OWN
    ).astype(BF16)

    pl.semaphore_wait(barrier, len(everyone))

    sends = []

    def remote(src, dst, send, recv, peer):
        copy = pltpu.make_async_remote_copy(
            src_ref=src, dst_ref=dst, send_sem=send, recv_sem=recv,
            device_id=peer, device_id_type=MESH,
        )
        copy.start()
        sends.append(copy)

    counter = [0]

    def gather_send(src, dst, n, peer):
        i = counter[0]
        counter[0] += 1
        remote(
            blocks.at[pl.ds(src, n)], blocks.at[pl.ds(dst, n)],
            g_send.at[i], g_recv.at[dst], peer,
        )

    def gather_wait(slot, n):
        pltpu.make_async_copy(
            blocks.at[pl.ds(slot, n)], blocks.at[pl.ds(slot, n)], g_recv.at[slot]
        ).wait()

    for d in (2, 1, 3):
        gather_send(0, BASE[0, 0] + ZS - d, 1, z_peer[d])
    gather_send(0, BASE[1, 0], 1, sibling)
    for d in (2, 1, 3):
        gather_send(0, BASE[0, XS - d], 1, x_peer[d])

    pts_t[WIDTH + 16 : 2 * WIDTH, :] = jnp.zeros((WIDTH - 16, npoints), BF16)
    row16 = lax.broadcasted_iota(jnp.int32, (16, WIDTH), 0)
    col16 = lax.broadcasted_iota(jnp.int32, (16, WIDTH), 1)
    eye16 = jnp.where(row16 == col16, 1.0, 0.0).astype(BF16)

    def prepare(j, carry):
        for u in range(4):
            at = pl.ds(pl.multiple_of((j * 4 + u) * WIDTH, WIDTH), WIDTH)
            x = points[at, :]
            xt = x.astype(F32).T
            half = -0.5 * jnp.sum(xt * xt, axis=0, keepdims=True)
            b_hi, b_mid, b_lo = split3(half)
            one = jnp.ones_like(half)
            tile = rows16({0: one, 1: one, 2: one, 3: b_hi, 4: b_mid, 5: b_lo}, WIDTH).astype(BF16)
            pts_t[0:WIDTH, at] = xt.astype(BF16)
            pts_t[WIDTH : WIDTH + 16, at] = tile
            pts[at, 0:WIDTH] = x
            pts[at, WIDTH : 2 * WIDTH] = lax.dot_general(
                tile, eye16, (((0,), (0,)), ((), ())), preferred_element_type=F32
            ).astype(BF16)
        return carry

    lax.fori_loop(0, npoints // WIDTH // 4, prepare, 0)

    for dz in (1, 3, 2):
        gather_wait(BASE[0, 0] + dz, 1)
        for d in (2, 1, 3):
            gather_send(dz, BASE[0, XS - d] + dz, 1, x_peer[d])
        gather_send(dz, BASE[1, 0] + dz, 1, sibling)

    row = lax.broadcasted_iota(jnp.int32, (16, 2 * WIDTH), 0)
    col = lax.broadcasted_iota(jnp.int32, (16, 2 * WIDTH), 1)
    put = ((row < 3) & (col == row)) | ((row == 6) & (col >= 3) & (col < 6))
    put = put | ((row >= 3) & (row < 6) & (col >= WIDTH))
    table = jnp.where(put, 1.0, 0.0).astype(BF16)

    def expand(first, n):
        for s in range(first, first + n):
            at = slice(s * OWN, (s + 1) * OWN)
            wide = spread_rows(blocks[s, OWN:BLOCK, :], table)[0:OWN, :]
            centres[at, 0:WIDTH] = blocks[s, 0:OWN, :]
            centres[at, WIDTH : 2 * WIDTH] = wide[:, 0:WIDTH].astype(BF16)
            scale[at, :] = wide[:, WIDTH : 2 * WIDTH]

    def first_pass(c):
        at = slice(c * CHUNK, (c + 1) * CHUNK)

        def half(h, carry):
            for t in range(npoints // TILE // 2):
                ns = pl.ds(pl.multiple_of(h * (npoints // 2) + t * TILE, TILE), TILE)
                y = jnp.dot(centres[at, :], pts_t[:, ns], preferred_element_type=F32)
                y = y * jnp.concatenate([scale[at, :]] * (TILE // WIDTH), axis=1)
                top = jnp.max(y, axis=0, keepdims=True)
                p = jnp.exp2(y - top)
                prob[at, ns] = p
                peak[c : c + 1, ns] = top
                mass[c : c + 1, ns] = jnp.sum(p, axis=0, keepdims=True)
            return carry

        lax.fori_loop(0, 2, half, 0)

    for dz in range(ZS):
        gather_wait(BASE[1, 0] + dz, 1)
    expand(0, 8)
    first_pass(0)
    for dx in (1, 3):
        for dz in range(ZS):
            gather_wait(BASE[0, dx] + dz, 1)
        gather_send(BASE[0, dx], BASE[1, dx], ZS, sibling)
    expand(8, 8)
    first_pass(1)
    for dz in range(ZS):
        gather_wait(BASE[0, 2] + dz, 1)
    gather_send(BASE[0, 2], BASE[1, 2], ZS, sibling)
    for dx in (1, 3):
        gather_wait(BASE[1, dx], ZS)
    expand(16, 8)
    first_pass(2)
    gather_wait(BASE[1, 2], ZS)
    expand(24, 8)
    first_pass(3)

    chunks = 4
    top = jnp.max(peak[0:chunks, :], axis=0, keepdims=True)
    total = jnp.sum(mass[0:chunks, :] * jnp.exp2(peak[0:chunks, :] - top), axis=0, keepdims=True)
    lse[0] = top + jnp.log(total) * LOG2E
    for d in range(1, comps):
        remote(lse.at[0], lse.at[comps - d], l_send.at[d], l_recv.at[comps - d], c_peer[d])
    for d in range(1, comps):
        pltpu.make_async_copy(lse.at[d], lse.at[d], l_recv.at[d]).wait()
    top = lse[0]
    for d in range(1, comps):
        top = jnp.maximum(top, lse[d])
    total = jnp.exp2(lse[0] - top)
    for d in range(1, comps):
        total = total + jnp.exp2(lse[d] - top)
    lik = top + jnp.log(total) * LOG2E
    out_lik[...] = lik * LN2
    for c in range(chunks):
        peak[c : c + 1, :] = jnp.exp2(peak[c : c + 1, :] - lik)

    def second_pass(c):
        at = slice(c * CHUNK, (c + 1) * CHUNK)
        acc = jnp.zeros((CHUNK, 2 * WIDTH), F32)
        for t in range(npoints // 1024):
            ns = slice(t * 1024, (t + 1) * 1024)
            p = (prob[at, ns] * peak[c : c + 1, ns]).astype(BF16)
            acc = acc + jnp.dot(p, pts[ns, :], preferred_element_type=F32)
        sums[at, :] = acc

    def span(first, n):
        return pl.ds(first * OWN, n * OWN)

    def to_sibling(i, dx, n):
        remote(
            sums.at[span(BASE[1, dx], n)], sib.at[span(SIB[dx], n)],
            r_send.at[i], r_recv.at[i], sibling,
        )

    def from_sibling(i, dx, n):
        ref = sib.at[span(SIB[dx], n)]
        pltpu.make_async_copy(ref, ref, r_recv.at[i]).wait()

    def stats_of(extra):
        t = extra.T
        return t[0:1, :], t[3:4, :] + t[4:5, :] + t[5:6, :]

    def pack_stats(cnt, sq):
        c_hi, c_mid, c_lo = split3(cnt)
        s_hi, s_mid, s_lo = split3(sq)
        parts = {0: c_hi, 1: c_mid, 2: c_lo, 3: s_hi, 4: s_mid, 5: s_lo}
        return rows16(parts, cnt.shape[1]).astype(BF16)

    def chip_sum(dx):
        a = slice(BASE[0, dx] * OWN, (BASE[0, dx] + ZS) * OWN)
        b = slice(SIB[dx] * OWN, (SIB[dx] + ZS) * OWN)
        return sums[a, :] + sib[b, :]

    span4 = ZS * OWN

    def to_x(dx):
        val = chip_sum(dx)
        cnt, sq = stats_of(val[:, WIDTH:])
        x_out[dx - 1, 0:span4, :] = val[:, 0:WIDTH].astype(BF16)
        tile = pack_stats(cnt, sq)
        x_out[dx - 1, span4 : span4 + 16, :] = tile[:, 0:WIDTH]
        x_out[dx - 1, span4 + 16 : span4 + 32, :] = tile[:, WIDTH:]
        remote(
            x_out.at[dx - 1], x_in.at[XS - dx - 1],
            r_send.at[3 + dx], r_recv.at[3 + XS - dx], x_peer[dx],
        )

    second_pass(3)
    to_sibling(0, 2, 4)
    second_pass(2)
    to_sibling(1, 1, 8)
    from_sibling(0, 2, 4)
    to_x(2)
    second_pass(1)
    from_sibling(1, 1, 8)
    to_x(1)
    to_x(3)
    second_pass(0)
    to_sibling(2, 0, 4)
    for dx in (1, 2, 3):
        ref = x_in.at[dx - 1]
        pltpu.make_async_copy(ref, ref, r_recv.at[3 + dx]).wait()
    from_sibling(2, 0, 4)

    val = chip_sum(0)
    tot = val[:, 0:WIDTH]
    cnt, sq = stats_of(val[:, WIDTH:])
    for i in range(XS - 1):
        tot = tot + x_in[i, 0:span4, :].astype(F32)
        tile = jnp.concatenate(
            [x_in[i, span4 : span4 + 16, :], x_in[i, span4 + 16 : span4 + 32, :]], axis=1
        ).astype(F32)
        cnt = cnt + tile[0:1, :] + tile[1:2, :] + tile[2:3, :]
        sq = sq + tile[3:4, :] + tile[4:5, :] + tile[5:6, :]
    tile = pack_stats(cnt, sq)
    for dz in (2, 1, 3):
        lanes = slice((dz // 2) * WIDTH, (dz // 2 + 1) * WIDTH)
        z_out[dz - 1, 0:OWN, :] = tot[dz * OWN : (dz + 1) * OWN, :].astype(BF16)
        z_out[dz - 1, OWN:BLOCK, :] = tile[:, lanes]
        remote(
            z_out.at[dz - 1], z_in.at[ZS - dz - 1],
            r_send.at[6 + dz], r_recv.at[6 + ZS - dz], z_peer[dz],
        )

    is_cnt = (row < 3) & (col < WIDTH)
    is_sq = (row >= 3) & (row < 6) & (col >= WIDTH)
    gather_stats = jnp.where(is_cnt | is_sq, 1.0, 0.0).astype(BF16)
    total = tot[0:OWN, :]
    stats = spread_rows(tile[:, 0:WIDTH], gather_stats)[0:OWN, :]
    for dz in (1, 3, 2):
        ref = z_in.at[dz - 1]
        pltpu.make_async_copy(ref, ref, r_recv.at[6 + dz]).wait()
    for dz in (1, 2, 3):
        half = ((ZS - dz) % 2) * OWN
        total = total + z_in[dz - 1, 0:OWN, :].astype(F32)
        stats = stats + spread_rows(z_in[dz - 1, OWN:BLOCK, :], gather_stats)[half : half + OWN, :]

    counts = stats[:, 0:WIDTH]
    squares = -2.0 * stats[:, WIDTH:]
    prior = means[...].astype(F32)
    prior_var = LOG2E / scale[0:OWN, :]
    denom = counts + 1.0
    centre = (total + prior) / denom
    cross = jnp.sum(centre * total, axis=1, keepdims=True)
    own_sq = jnp.sum(centre * centre, axis=1, keepdims=True)
    spread = (squares - 2.0 * cross + counts * own_sq + WIDTH * prior_var) / (WIDTH * denom)
    weight = jnp.log(denom / (total_points + COMPONENTS))
    out_means[...] = centre.astype(BF16)
    lane = lax.broadcasted_iota(jnp.int32, (OWN, WIDTH), 1)
    flat = jnp.where(lane == 0, spread, weight).T
    out_var[...] = flat[0:1, :]
    out_logw[...] = flat[1:2, :]

    for copy in sends:
        copy.wait_send()


def per_device(points, means, variances, log_weights):
    comps = lax.axis_size("comp")
    npoints = points.shape[0]
    own = means.shape[0]
    group = own * lax.axis_size("dp")
    vmem = pl.BlockSpec(memory_space=pltpu.VMEM)
    shape = jax.ShapeDtypeStruct
    new_means, new_var, new_logw, lik = pl.pallas_call(
        functools.partial(body, comps, npoints, npoints * lax.axis_size("dp")),
        out_shape=[
            shape((own, WIDTH), BF16),
            shape((1, own), F32),
            shape((1, own), F32),
            shape((1, npoints), F32),
        ],
        in_specs=[vmem] * 4,
        out_specs=[vmem] * 4,
        scratch_shapes=[
            pltpu.VMEM((32, BLOCK, WIDTH), BF16),
            pltpu.VMEM((group, 2 * WIDTH), BF16),
            pltpu.VMEM((group, WIDTH), F32),
            pltpu.VMEM((2 * WIDTH, npoints), BF16),
            pltpu.VMEM((npoints, 2 * WIDTH), BF16),
            pltpu.VMEM((group, npoints), F32),
            pltpu.VMEM((8, npoints), F32),
            pltpu.VMEM((8, npoints), F32),
            pltpu.VMEM((comps, 1, npoints), F32),
            pltpu.VMEM((group, 2 * WIDTH), F32),
            pltpu.VMEM((group // 2, 2 * WIDTH), F32),
            pltpu.VMEM((3, 4 * OWN + 32, WIDTH), BF16),
            pltpu.VMEM((3, 4 * OWN + 32, WIDTH), BF16),
            pltpu.VMEM((3, BLOCK, WIDTH), BF16),
            pltpu.VMEM((3, BLOCK, WIDTH), BF16),
            pltpu.SemaphoreType.DMA((32,)),
            pltpu.SemaphoreType.DMA((32,)),
            pltpu.SemaphoreType.DMA((8,)),
            pltpu.SemaphoreType.DMA((8,)),
            pltpu.SemaphoreType.DMA((10,)),
            pltpu.SemaphoreType.DMA((10,)),
        ],
        compiler_params=pltpu.CompilerParams(
            collective_id=0, has_side_effects=True, vmem_limit_bytes=60 << 20
        ),
        name="em_step",
    )(points, means, variances.reshape(1, own), log_weights.reshape(1, own))
    return new_means, new_var.reshape(own), new_logw.reshape(own), lik.reshape(npoints)


def solution(mesh):
    in_specs = (P("dp", None), P(("dp", "comp"), None), P(("dp", "comp")), P(("dp", "comp")))
    out_specs = (P(("dp", "comp"), None), P(("dp", "comp")), P(("dp", "comp")), P("dp"))
    return jax.shard_map(
        per_device, mesh=mesh, in_specs=in_specs, out_specs=out_specs, check_vma=False
    )
```

time: 679 us -> 55.9 us (0.08)
  blocking collectives: 386 us -> 0 us
  waiting for transfers between devices: 144 us -> 0 us
  matrix products: 100 us -> 0 us
  Pallas kernels: 0 us -> 51.9 us
  local copies, waits for them, and re-layouts: 21.7 us -> 3.13 us
  between operations: 14.8 us -> 0.66 us
  other arithmetic: 10.7 us -> 0 us
    psum x2 -> x0, blocking collectives: 177 us -> none  [the longest x1 152 us: per_device(): sums, counts, squares = lax.psum((sums, counts, squares), 'dp')]
    psum x1 -> x0, waiting for transfers between devices: 144 us -> none  [per_device(): sums, counts, squares = lax.psum((sums, counts, squares), 'dp')]
    unnamed x1 -> x0, blocking collectives: 132 us -> none
    dot_general x32 -> x0, matrix products: 100 us -> none  [the longest x8 48.3 us: second_pass(): lax.dot_general(prob, block.astype(jnp.float32), (((0,), (0,)), ((), ()))...]
    pallas_call x0 -> x1, Pallas kernels: none -> 51.9 us  [per_device(): pl.pallas_call(functools.partial(body, comps, npoints, npoints * lax.axis...]
    all_gather x1 -> x0, blocking collectives: 50.4 us -> none  [per_device(): centres = lax.all_gather(means, 'dp', axis=0, tiled=True)]
    pmax x1 -> x0, blocking collectives: 27.1 us -> none  [per_device(): row_peak = lax.pmax(local_peak, 'comp')]
    while x16 -> x0, local copies, waits for them, and re-layouts: 15.3 us -> none
  transfers between devices with their start and end apart: 1 -> 0, of which waited for: 1 -> 0; matrix products, arithmetic and copies ran while one was open for 0% -> 0% of each run, Pallas kernels for 0% -> 0%
where the time goes in v1:
time: 55.9 us; the launch traced here: 55.7 us
  Pallas kernels  51.9 us (93%)
  local copies, waits for them, and re-layouts  3.13 us (6%)
  between operations  0.66 us (1%)
    pallas_call x1, Pallas kernels, per_device(): pl.pallas_call(functools.partial(body, comps, npoints, npoints * lax.axis...  51.9 us
    unnamed x10, local copies, waits for them, and re-layouts  3.13 us

profile of v1, /device:TPU:1, one launch (start us, length us, event | category | flops | bytes accessed | tf_op | source)
XLA Modules:
  0.0 55.7 jit_solution(10558696026563518563)
XLA Ops:
  0.6 51.9 %em_step.1 = (bf16[64,128]{1,0:T(8,128)(2,1)}, f32[1,64]{1,0:T(1,128)}, f32[1,64]{1,0:T(1,128)}, f32[1,4096]{1,0:T(1,128)}) custom-call(bf16[4096,128]{1,0:T(8,128)(2,1)} %points.1, bf16[64,128]{1,0:T(8,128)(2,1)} %means.1, f32[1,64]{1,0:T(1,128)} %bitcast.6, f32[1,64]{1,0:T(1,128)} %bitcast.7), custom_call_target="tpu_custom_call" | custom-call | tf_op jit(solution)/shard_map/em_step/pallas_call | solution.py:368
  52.6 0.0 copy-start.2
  52.6 0.0 copy-start
  52.6 1.3 %copy.12 = bf16[64,128]{1,0:T(8,128)(2,1)} copy(bf16[64,128]{1,0:T(8,128)(2,1)} %get-tuple-element.16) | data formatting | bytes 32768
  53.9 0.0 copy-done.2
  53.9 0.0 copy-start.1
  53.9 0.5 copy.13
  54.4 0.2 copy-done.1
  54.6 0.5 copy.14
  55.1 0.0 copy-done
  55.1 0.6 %copy.15 = f32[4096]{0:T(1024)} copy(f32[4096]{0:T(1024)S(1)} %bitcast.5) | data formatting | bytes 32768
Async XLA Ops:
  52.6 1.4 %copy-start.2 = (f32[1,64]{1,0:T(1,128)S(1)}, f32[1,64]{1,0:T(1,128)}, u32[]{:S(2)}) copy-start(f32[1,64]{1,0:T(1,128)} %get-tuple-element.9) | copy-start | bytes 772
  52.6 2.5 %copy-start = (f32[1,4096]{1,0:T(1,128)S(1)}, f32[1,4096]{1,0:T(1,128)}, u32[]{:S(2)}) copy-start(f32[1,4096]{1,0:T(1,128)} %get-tuple-element.11) | copy-start | bytes 49156
  53.9 0.7 %copy-start.1 = (f32[1,64]{1,0:T(1,128)S(1)}, f32[1,64]{1,0:T(1,128)}, u32[]{:S(2)}) copy-start(f32[1,64]{1,0:T(1,128)} %get-tuple-element.10) | copy-start | bytes 772

commit v2 on v1

v2 whole, which is shorter than its diff:
```python
import functools

import jax
import jax.numpy as jnp
from jax import lax
from jax.experimental import pallas as pl
from jax.experimental.pallas import tpu as pltpu
from jax.sharding import PartitionSpec as P

MESH = pl.DeviceIdType.MESH
F32 = jnp.float32
BF16 = jnp.bfloat16

COMPONENTS = 16384
LOG2E = 1.4426950408889634
LN2 = 0.6931471805599453
TWO_PI = 6.283185307179586

XS, ZS, CORES = 4, 4, 2
Z = 8
DEPTH = 4
WIDTH = 128
OWN = 64
BLOCK = 80
CHUNK = 512
TILE = 512
PARTS = 4

BASE = {
    (0, 0): 0, (1, 0): 4,
    (0, 1): 8, (0, 2): 12,
    (1, 1): 16, (1, 2): 20,
    (0, 3): 24, (1, 3): 28,
}
GROUP = XS * OWN


def split3(v):
    hi = v.astype(BF16).astype(F32)
    mid = (v - hi).astype(BF16).astype(F32)
    lo = (v - hi - mid).astype(BF16).astype(F32)
    return hi, mid, lo


def rows16(parts, lanes):
    row = lax.broadcasted_iota(jnp.int32, (16, lanes), 0)
    out = jnp.zeros((16, lanes), F32)
    for i, part in parts.items():
        out = jnp.where(row == i, jnp.broadcast_to(part, (16, lanes)), out)
    return out


def spread_rows(tile, table):
    return lax.dot_general(tile, table, (((0,), (0,)), ((), ())), preferred_element_type=F32)


def body(
    comps, npoints, total_points,
    points_hbm, means_hbm, var_hbm, logw_hbm,
    out_means, out_var, out_logw, out_lik,
    points, means, var, logw, blocks, centres, scale, pts_t, pts, prob, peak, mass, lse, sums,
    sib_out, sib, sib_stats_out, sib_stats, r_out, r_in,
    p_sem, g_send, g_recv, l_send, l_recv, s_send, s_recv, r_send, r_recv,
):
    dp = lax.axis_index("dp")
    cp = lax.axis_index("comp")
    core = dp % CORES
    zh = (dp // CORES) % ZS
    xx = dp // (CORES * ZS)
    zl = cp % 2
    yy = cp // 2
    zz = zh * 2 + zl
    sign = 1 - 2 * zl

    def device(dx, dz, dc=0):
        z = (zz + dz + Z) % Z
        return {
            "dp": ((xx + dx) % XS) * (ZS * CORES) + (z // 2) * CORES + (core + dc) % CORES,
            "comp": yy * 2 + z % 2,
        }

    def owner(dx, j, dc=0):
        return device(dx, -sign * j, dc)

    def user(dx, j, dc=0):
        return device(XS - dx, sign * j if j % 2 == 0 else -sign * j, dc)

    sibling = {"dp": dp + 1 - 2 * core}
    c_peer = {d: {"comp": (cp + d) % comps} for d in range(1, comps)}
    others = [(dx, j) for j in range(DEPTH) for dx in range(XS) if (dx, j) != (0, 0)]

    barrier = pltpu.get_barrier_semaphore()
    everyone = [sibling, *c_peer.values()]
    everyone += [owner(dx, j) for dx, j in others]
    everyone += [user(dx, 2) for dx in range(XS)]
    everyone += [owner(dx, 0, 1) for dx in range(1, XS)]
    for peer in everyone:
        pl.semaphore_signal(barrier, inc=1, device_id=peer, device_id_type=MESH)
    fetches = [
        pltpu.make_async_copy(src, dst, p_sem.at[i])
        for i, (src, dst) in enumerate(
            [(means_hbm, means), (var_hbm, var), (logw_hbm, logw), (points_hbm, points)]
        )
    ]
    for copy in fetches:
        copy.start()
    for copy in fetches[:3]:
        copy.wait()

    m = means[...]
    mf = m.astype(F32)
    msq = mf * mf
    msq_hi = msq.astype(BF16)
    msq_lo = (msq - msq_hi.astype(F32)).astype(BF16)
    ones = jnp.ones((16, WIDTH), BF16)
    nt = (((1,), (1,)), ((), ()))
    centre_sq = (
        lax.dot_general(ones, msq_hi, nt, preferred_element_type=F32)
        + lax.dot_general(ones, msq_lo, nt, preferred_element_type=F32)
    )[0:1, :]
    v = var[...]
    offset = logw[...] - 0.5 * WIDTH * jnp.log(TWO_PI * v)
    e_hi, e_mid, e_lo = split3(v * offset - 0.5 * centre_sq)
    a_hi, a_mid, a_lo = split3(LOG2E / v)
    blocks[0, 0:OWN, :] = m
    blocks[0, OWN:BLOCK, :] = jnp.zeros((16, WIDTH), BF16)
    blocks[0, OWN:BLOCK, 0:OWN] = rows16(
        {0: e_hi, 1: e_mid, 2: e_lo, 3: a_hi, 4: a_mid, 5: a_lo, 6: jnp.ones_like(v)}, OWN
    ).astype(BF16)

    pts_t[WIDTH + 16 : 2 * WIDTH, :] = jnp.zeros((WIDTH - 16, npoints), BF16)
    row16 = lax.broadcasted_iota(jnp.int32, (16, WIDTH), 0)
    col16 = lax.broadcasted_iota(jnp.int32, (16, WIDTH), 1)
    eye16 = jnp.where(row16 == col16, 1.0, 0.0).astype(BF16)

    def prepare(j, carry):
        for u in range(4):
            at = pl.ds(pl.multiple_of((j * 4 + u) * WIDTH, WIDTH), WIDTH)
            x = points[at, :]
            xt = x.astype(F32).T
            half = -0.5 * jnp.sum(xt * xt, axis=0, keepdims=True)
            b_hi, b_mid, b_lo = split3(half)
            one = jnp.ones_like(half)
            tile = rows16({0: one, 1: one, 2: one, 3: b_hi, 4: b_mid, 5: b_lo}, WIDTH).astype(BF16)
            pts_t[0:WIDTH, at] = xt.astype(BF16)
            pts_t[WIDTH : WIDTH + 16, at] = tile
            pts[at, 0:WIDTH] = x
            pts[at, WIDTH : 2 * WIDTH] = lax.dot_general(
                tile, eye16, (((0,), (0,)), ((), ())), preferred_element_type=F32
            ).astype(BF16)
        return carry

    fetches[3].wait()
    steps = npoints // WIDTH // 4
    lax.fori_loop(0, steps // 2, prepare, 0)

    pl.semaphore_wait(barrier, len(everyone))

    sends = []

    def remote(src, dst, send, recv, peer):
        copy = pltpu.make_async_remote_copy(
            src_ref=src, dst_ref=dst, send_sem=send, recv_sem=recv,
            device_id=peer, device_id_type=MESH,
        )
        copy.start()
        sends.append(copy)

    def arrived(ref, sem):
        pltpu.make_async_copy(ref, ref, sem).wait()

    counter = [0]

    def gather_send(src, dst, n, peer):
        i = counter[0]
        counter[0] += 1
        remote(
            blocks.at[pl.ds(src, n)], blocks.at[pl.ds(dst, n)],
            g_send.at[i], g_recv.at[dst], peer,
        )

    def gather_wait(slot, n):
        arrived(blocks.at[pl.ds(slot, n)], g_recv.at[slot])

    gather_send(0, BASE[1, 0], 1, sibling)
    for dx in (2, 1, 3):
        gather_send(0, BASE[0, 0] + dx, 1, user(dx, 0))
        gather_send(0, BASE[1, 0] + dx, 1, user(dx, 0, 1))
    for j in (1, 2, 3):
        for dx in (2, 1, 3, 0):
            gather_send(0, BASE[0, j] + dx, 1, user(dx, j))

    lax.fori_loop(steps // 2, steps, prepare, 0)

    row = lax.broadcasted_iota(jnp.int32, (16, 2 * WIDTH), 0)
    col = lax.broadcasted_iota(jnp.int32, (16, 2 * WIDTH), 1)
    put = ((row < 3) & (col == row)) | ((row == 6) & (col >= 3) & (col < 6))
    put = put | ((row >= 3) & (row < 6) & (col >= WIDTH))
    table = jnp.where(put, 1.0, 0.0).astype(BF16)

    def expand(first, n):
        for s in range(first, first + n):
            at = slice(s * OWN, (s + 1) * OWN)
            wide = spread_rows(blocks[s, OWN:BLOCK, :], table)[0:OWN, :]
            centres[at, 0:WIDTH] = blocks[s, 0:OWN, :]
            centres[at, WIDTH : 2 * WIDTH] = wide[:, 0:WIDTH].astype(BF16)
            scale[at, :] = wide[:, WIDTH : 2 * WIDTH]

    def first_pass(c, first, last):
        at = slice(c * CHUNK, (c + 1) * CHUNK)
        for t in range(first // TILE, last // TILE):
            ns = slice(t * TILE, (t + 1) * TILE)
            y = jnp.dot(centres[at, :], pts_t[:, ns], preferred_element_type=F32)
            y = y * jnp.concatenate([scale[at, :]] * (TILE // WIDTH), axis=1)
            top = jnp.max(y, axis=0, keepdims=True)
            p = jnp.exp2(y - top)
            prob[at, ns] = p
            peak[c : c + 1, ns] = top
            mass[c : c + 1, ns] = jnp.sum(p, axis=0, keepdims=True)

    chunks = 4
    part = npoints // PARTS
    parts = [slice(h * part, (h + 1) * part) for h in range(PARTS)]

    def lse_send(h):
        ns = parts[h]
        top = jnp.max(peak[0:chunks, ns], axis=0, keepdims=True)
        total = jnp.sum(mass[0:chunks, ns] * jnp.exp2(peak[0:chunks, ns] - top), axis=0, keepdims=True)
        lse[h, 0] = top + jnp.log(total) * LOG2E
        for d in range(1, comps):
            remote(
                lse.at[h, 0], lse.at[h, comps - d],
                l_send.at[h, d], l_recv.at[h, comps - d], c_peer[d],
            )

    def lse_finish(h):
        ns = parts[h]
        for d in range(1, comps):
            arrived(lse.at[h, d], l_recv.at[h, d])
        top = lse[h, 0]
        for d in range(1, comps):
            top = jnp.maximum(top, lse[h, d])
        total = jnp.exp2(lse[h, 0] - top)
        for d in range(1, comps):
            total = total + jnp.exp2(lse[h, d] - top)
        lik = top + jnp.log(total) * LOG2E
        out_lik[:, ns] = lik * LN2
        for c in range(chunks):
            peak[c : c + 1, ns] = jnp.exp2(peak[c : c + 1, ns] - lik)

    for dx in range(XS):
        if dx:
            gather_wait(BASE[0, 0] + dx, 1)
        gather_wait(BASE[1, 0] + dx, 1)
    expand(0, 8)
    first_pass(0, 0, npoints)
    for j in (1, 2):
        for dx in range(XS):
            gather_wait(BASE[0, j] + dx, 1)
        gather_send(BASE[0, j], BASE[1, j], XS, sibling)
    expand(8, 8)
    first_pass(1, 0, npoints)
    for dx in range(XS):
        gather_wait(BASE[0, 3] + dx, 1)
    gather_send(BASE[0, 3], BASE[1, 3], XS, sibling)
    gather_wait(BASE[1, 1], XS)
    gather_wait(BASE[1, 2], XS)
    expand(16, 12)
    for h in range(PARTS):
        first_pass(2, parts[h].start, parts[h].stop)
        if h == 0:
            gather_wait(BASE[1, 3], XS)
            expand(28, 4)
        first_pass(3, parts[h].start, parts[h].stop)
        lse_send(h)

    def second_pass(h, groups):
        ns = parts[h]
        p = []
        for g in groups:
            first = BASE[g] * OWN
            c = first // CHUNK
            p.append((prob[first : first + GROUP, ns] * peak[c : c + 1, ns]).astype(BF16))
        acc = jnp.dot(jnp.concatenate(p, axis=0), pts[ns, :], preferred_element_type=F32)
        for i, g in enumerate(groups):
            at = slice(BASE[g] * OWN, BASE[g] * OWN + GROUP)
            val = acc[i * GROUP : (i + 1) * GROUP, :]
            val = val if h == 0 else sums[at, :] + val
            sums[at, :] = val
            if h == PARTS - 1 and g[0] == 1:
                sib_out[g[1]] = val[:, 0:WIDTH]
                sib_stats_out[g[1]] = val[:, WIDTH:].T[0:8, :]

    def to_sibling(j):
        remote(sib_out.at[j], sib.at[j], s_send.at[0, j], s_recv.at[0, j], sibling)
        remote(sib_stats_out.at[j], sib_stats.at[j], s_send.at[1, j], s_recv.at[1, j], sibling)

    def pack_stats(cnt, sq):
        c_hi, c_mid, c_lo = split3(cnt)
        s_hi, s_mid, s_lo = split3(sq)
        parts = {0: c_hi, 1: c_mid, 2: c_lo, 3: s_hi, 4: s_mid, 5: s_lo}
        return rows16(parts, cnt.shape[1]).astype(BF16)

    def chip_sum(j):
        at = slice(BASE[0, j] * OWN, BASE[0, j] * OWN + GROUP)
        t = sums[at, WIDTH:].T[0:8, :]
        arrived(sib.at[j], s_recv.at[0, j])
        arrived(sib_stats.at[j], s_recv.at[1, j])
        t = t + sib_stats[j]
        return sums[at, 0:WIDTH] + sib[j], t[0:1, :], t[3:4, :] + t[4:5, :] + t[5:6, :]

    def to_owner(j):
        tot, cnt, sq = chip_sum(j)
        tile = pack_stats(cnt, sq)
        for dx in (2, 1, 3, 0):
            if (dx, j) == (0, 0):
                continue
            r_out[j, dx, 0:OWN, :] = tot[dx * OWN : (dx + 1) * OWN, :].astype(BF16)
            r_out[j, dx, OWN:BLOCK, :] = tile[:, (dx // 2) * WIDTH : (dx // 2 + 1) * WIDTH]
            remote(
                r_out.at[j, dx], r_in.at[j, dx], r_send.at[j, dx], r_recv.at[j, dx], owner(dx, j)
            )
        return tot[0:OWN, :], cnt[:, 0:WIDTH], sq[:, 0:WIDTH]

    steps = [[(1, 3), (1, 2)], [(1, 1), (1, 0)], [(0, 3), (0, 2)], [(0, 1), (0, 0)]]
    for h in range(PARTS - 1):
        lse_finish(h)
        for step in steps:
            second_pass(h, step)
    lse_finish(PARTS - 1)
    second_pass(PARTS - 1, steps[0])
    to_sibling(3)
    to_sibling(2)
    second_pass(PARTS - 1, steps[1])
    to_sibling(1)
    to_sibling(0)
    second_pass(PARTS - 1, steps[2])
    second_pass(PARTS - 1, steps[3])
    to_owner(3)
    to_owner(2)
    to_owner(1)
    total, cnt, sq = to_owner(0)

    tiles = [None, None]
    for dx, j in sorted(others, key=lambda o: -o[1]):
        arrived(r_in.at[j, dx], r_recv.at[j, dx])
        total = total + r_in[j, dx, 0:OWN, :].astype(F32)
        tile = r_in[j, dx, OWN:BLOCK, :].astype(F32)
        tiles[dx % 2] = tile if tiles[dx % 2] is None else tiles[dx % 2] + tile
    is_cnt = (row < 3) & (col < WIDTH)
    is_sq = (row >= 3) & (row < 6) & (col >= WIDTH)
    columns = jnp.where(is_cnt | is_sq, 1.0, 0.0).astype(BF16)
    stats = 0.0
    for odd in (0, 1):
        t = tiles[odd]
        c = t[0:1, :] + t[1:2, :] + t[2:3, :]
        s = t[3:4, :] + t[4:5, :] + t[5:6, :]
        if not odd:
            c, s = c + cnt, s + sq
        wide = spread_rows(pack_stats(c, s), columns)
        stats = stats + wide[odd * OWN : (odd + 1) * OWN, :]

    counts = stats[:, 0:WIDTH]
    squares = -2.0 * stats[:, WIDTH:]
    prior = means[...].astype(F32)
    prior_var = LOG2E / scale[0:OWN, :]
    denom = counts + 1.0
    centre = (total + prior) / denom
    cross = jnp.sum(centre * total, axis=1, keepdims=True)
    own_sq = jnp.sum(centre * centre, axis=1, keepdims=True)
    spread = (squares - 2.0 * cross + counts * own_sq + WIDTH * prior_var) / (WIDTH * denom)
    weight = jnp.log(denom / (total_points + COMPONENTS))
    out_means[...] = centre.astype(BF16)
    lane = lax.broadcasted_iota(jnp.int32, (OWN, WIDTH), 1)
    flat = jnp.where(lane == 0, spread, weight).T
    out_var[...] = flat[0:1, :]
    out_logw[...] = flat[1:2, :]

    for copy in sends:
        copy.wait_send()


def finish(*refs):
    for src, dst in zip(refs[:4], refs[4:]):
        dst[...] = src[...]


def per_device(points, means, variances, log_weights):
    comps = lax.axis_size("comp")
    npoints = points.shape[0]
    own = means.shape[0]
    group = own * lax.axis_size("dp")
    vmem = pl.BlockSpec(memory_space=pltpu.VMEM)
    shape = jax.ShapeDtypeStruct
    dma = pltpu.SemaphoreType.DMA
    results = pl.pallas_call(
        functools.partial(body, comps, npoints, npoints * lax.axis_size("dp")),
        out_shape=[
            shape((own, WIDTH), BF16),
            shape((1, own), F32),
            shape((1, own), F32),
            shape((1, npoints), F32),
        ],
        in_specs=[pl.BlockSpec(memory_space=pl.ANY)] * 4,
        out_specs=[vmem] * 4,
        scratch_shapes=[
            pltpu.VMEM((npoints, WIDTH), BF16),
            pltpu.VMEM((own, WIDTH), BF16),
            pltpu.VMEM((1, own), F32),
            pltpu.VMEM((1, own), F32),
            pltpu.VMEM((32, BLOCK, WIDTH), BF16),
            pltpu.VMEM((group, 2 * WIDTH), BF16),
            pltpu.VMEM((group, WIDTH), F32),
            pltpu.VMEM((2 * WIDTH, npoints), BF16),
            pltpu.VMEM((npoints, 2 * WIDTH), BF16),
            pltpu.VMEM((group, npoints), F32),
            pltpu.VMEM((8, npoints), F32),
            pltpu.VMEM((8, npoints), F32),
            pltpu.VMEM((PARTS, comps, 1, npoints // PARTS), F32),
            pltpu.VMEM((group, 2 * WIDTH), F32),
            pltpu.VMEM((DEPTH, GROUP, WIDTH), F32),
            pltpu.VMEM((DEPTH, GROUP, WIDTH), F32),
            pltpu.VMEM((DEPTH, 8, GROUP), F32),
            pltpu.VMEM((DEPTH, 8, GROUP), F32),
            pltpu.VMEM((DEPTH, XS, BLOCK, WIDTH), BF16),
            pltpu.VMEM((DEPTH, XS, BLOCK, WIDTH), BF16),
            dma((4,)),
            dma((32,)),
            dma((32,)),
            dma((PARTS, comps)),
            dma((PARTS, comps)),
            dma((2, DEPTH)),
            dma((2, DEPTH)),
            dma((DEPTH, XS)),
            dma((DEPTH, XS)),
        ],
        compiler_params=pltpu.CompilerParams(
            collective_id=0, has_side_effects=True, vmem_limit_bytes=60 << 20
        ),
        name="em_step",
    )(points, means, variances.reshape(1, own), log_weights.reshape(1, own))
    new_means, new_var, new_logw, lik = pl.pallas_call(
        finish,
        out_shape=[
            shape((own, WIDTH), BF16),
            shape((1, own), F32),
            shape((1, own), F32),
            shape((1, npoints), F32),
        ],
        in_specs=[vmem] * 4,
        out_specs=[vmem] * 4,
        name="results",
    )(*results)
    return new_means, new_var.reshape(own), new_logw.reshape(own), lik.reshape(npoints)


def solution(mesh):
    in_specs = (P("dp", None), P(("dp", "comp"), None), P(("dp", "comp")), P(("dp", "comp")))
    out_specs = (P(("dp", "comp"), None), P(("dp", "comp")), P(("dp", "comp")), P("dp"))
    return jax.shard_map(
        per_device, mesh=mesh, in_specs=in_specs, out_specs=out_specs, check_vma=False
    )
```

time: 55.9 us -> 48.2 us (0.86)
  Pallas kernels: 51.9 us -> 47.4 us
  local copies, waits for them, and re-layouts: 3.13 us -> 0 us
    pallas_call x1, Pallas kernels: 51.9 us -> 46 us  [per_device(): pl.pallas_call(functools.partial(body, comps, npoints, npoints * lax.axis...]
    unnamed x10 -> x0, local copies, waits for them, and re-layouts: 3.13 us -> none
    pallas_call x0 -> x1, Pallas kernels: none -> 1.37 us  [per_device(): pl.pallas_call(finish, out_shape=[shape((own, WIDTH), BF16), shape((1, ow...]
where the time goes in v2:
time: 48.2 us; the launch traced here: 48 us
  Pallas kernels  47.4 us (98%)
  between operations  0.64 us (1%)
    pallas_call x1, Pallas kernels, per_device(): pl.pallas_call(functools.partial(body, comps, npoints, npoints * lax.axis...  46 us
    pallas_call x1, Pallas kernels, per_device(): pl.pallas_call(finish, out_shape=[shape((own, WIDTH), BF16), shape((1, ow...  1.37 us

profile of v2, /device:TPU:1, one launch (start us, length us, event | category | flops | bytes accessed | tf_op | source)
XLA Modules:
  0.0 48.0 jit_solution(13366157884291313395)
XLA Ops:
  0.6 46.0 %em_step.1 = (bf16[64,128]{1,0:T(8,128)(2,1)}, f32[1,64]{1,0:T(1,128)}, f32[1,64]{1,0:T(1,128)}, f32[1,4096]{1,0:T(1,128)}) custom-call(bf16[4096,128]{1,0:T(8,128)(2,1)} %points_hbm.1, bf16[64,128]{1,0:T(8,128)(2,1)} %means_hbm.1, f32[1,64]{1,0:T(1,128)} %bitcast.5, f32[1,64]{1,0:T(1,128)} %bitcast.6), custom_call_target="tpu_custom_call" | custom-call | tf_op jit(solution)/shard_map/em_step/pallas_call | solution.py:396
  46.6 1.4 %results.1 = (bf16[64,128]{1,0:T(8,128)(2,1)}, f32[1,64]{1,0:T(1,128)}, f32[1,64]{1,0:T(1,128)}, f32[1,4096]{1,0:T(1,128)}) custom-call(bf16[64,128]{1,0:T(8,128)(2,1)} %get-tuple-element.12.refs_0_, f32[1,64]{1,0:T(1,128)} %get-tuple-element.13.refs_1_, f32[1,64]{1,0:T(1,128)} %get-tuple-element.14.refs_2_, f32[1,4096]{1,0:T(1,128)} %get-tuple-element.15.refs_3_), custom_call_target="tpu_custom_call" | custom-call | tf_op jit(solution)/shard_map/results/pallas_call | solution.py:442

commit v3 on v2

--- a/solution.py
+++ b/solution.py
@@ -24,7 +24,7 @@
 BLOCK = 80
 CHUNK = 512
 TILE = 512
-PARTS = 4
+PARTS = 2
 
 BASE = {
     (0, 0): 0, (1, 0): 4,
@@ -87,7 +87,9 @@
 
     sibling = {"dp": dp + 1 - 2 * core}
     c_peer = {d: {"comp": (cp + d) % comps} for d in range(1, comps)}
-    others = [(dx, j) for j in range(DEPTH) for dx in range(XS) if (dx, j) != (0, 0)]
+    others = [(dx, j) for j in range(DEPTH - 1) for dx in range(XS) if (dx, j) != (0, 0)]
+    far = DEPTH - 1
+    others.append((0, far))
 
     barrier = pltpu.get_barrier_semaphore()
     everyone = [sibling, *c_peer.values()]
@@ -186,7 +188,8 @@
     for dx in (2, 1, 3):
         gather_send(0, BASE[0, 0] + dx, 1, user(dx, 0))
         gather_send(0, BASE[1, 0] + dx, 1, user(dx, 0, 1))
-    for j in (1, 2, 3):
+    gather_send(0, BASE[0, far], 1, user(0, far))
+    for j in (1, 2):
         for dx in (2, 1, 3, 0):
             gather_send(0, BASE[0, j] + dx, 1, user(dx, j))
 
@@ -254,22 +257,25 @@
         gather_wait(BASE[1, 0] + dx, 1)
     expand(0, 8)
     first_pass(0, 0, npoints)
+    gather_wait(BASE[0, far], 1)
+    for d in (2, 1, 3):
+        gather_send(BASE[0, far], BASE[0, far] + XS - d, 1, device(d, 0))
     for j in (1, 2):
         for dx in range(XS):
             gather_wait(BASE[0, j] + dx, 1)
         gather_send(BASE[0, j], BASE[1, j], XS, sibling)
     expand(8, 8)
     first_pass(1, 0, npoints)
-    for dx in range(XS):
-        gather_wait(BASE[0, 3] + dx, 1)
-    gather_send(BASE[0, 3], BASE[1, 3], XS, sibling)
+    for dx in range(1, XS):
+        gather_wait(BASE[0, far] + dx, 1)
+    gather_send(BASE[0, far], BASE[1, far], XS, sibling)
     gather_wait(BASE[1, 1], XS)
     gather_wait(BASE[1, 2], XS)
     expand(16, 12)
     for h in range(PARTS):
         first_pass(2, parts[h].start, parts[h].stop)
         if h == 0:
-            gather_wait(BASE[1, 3], XS)
+            gather_wait(BASE[1, far], XS)
             expand(28, 4)
         first_pass(3, parts[h].start, parts[h].stop)
         lse_send(h)
@@ -309,20 +315,44 @@
         t = t + sib_stats[j]
         return sums[at, 0:WIDTH] + sib[j], t[0:1, :], t[3:4, :] + t[4:5, :] + t[5:6, :]
 
+    def packet(j, dx, tot, tile):
+        r_out[j, dx, 0:OWN, :] = tot.astype(BF16)
+        r_out[j, dx, OWN:BLOCK, :] = tile
+
+    def send_packet(j, dx, slot, peer):
+        remote(r_out.at[j, dx], r_in.at[j, slot], r_send.at[j, dx], r_recv.at[j, slot], peer)
+
     def to_owner(j):
         tot, cnt, sq = chip_sum(j)
         tile = pack_stats(cnt, sq)
         for dx in (2, 1, 3, 0):
-            if (dx, j) == (0, 0):
+            if dx == 0 and j in (0, far):
                 continue
-            r_out[j, dx, 0:OWN, :] = tot[dx * OWN : (dx + 1) * OWN, :].astype(BF16)
-            r_out[j, dx, OWN:BLOCK, :] = tile[:, (dx // 2) * WIDTH : (dx // 2 + 1) * WIDTH]
-            remote(
-                r_out.at[j, dx], r_in.at[j, dx], r_send.at[j, dx], r_recv.at[j, dx], owner(dx, j)
-            )
+            lanes = slice((dx // 2) * WIDTH, (dx // 2 + 1) * WIDTH)
+            packet(j, dx, tot[dx * OWN : (dx + 1) * OWN, :], tile[:, lanes])
+            if j == far:
+                send_packet(j, dx, XS - dx, device(dx, 0))
+            else:
+                send_packet(j, dx, dx, owner(dx, j))
         return tot[0:OWN, :], cnt[:, 0:WIDTH], sq[:, 0:WIDTH]
 
-    steps = [[(1, 3), (1, 2)], [(1, 1), (1, 0)], [(0, 3), (0, 2)], [(0, 1), (0, 0)]]
+    def rows_of(tile):
+        t = tile.astype(F32)
+        return t[0:1, :] + t[1:2, :] + t[2:3, :], t[3:4, :] + t[4:5, :] + t[5:6, :]
+
+    def add_packets(total, even, odd, slots):
+        even, odd = list(even), [jnp.zeros_like(e) if odd is None else o for e, o in zip(even, odd or even)]
+        for j, dx in slots:
+            arrived(r_in.at[j, dx], r_recv.at[j, dx])
+            total = total + r_in[j, dx, 0:OWN, :].astype(F32)
+            got = rows_of(r_in[j, dx, OWN:BLOCK, :])
+            if dx % 2 == 0:
+                even = [a + b for a, b in zip(even, got)]
+            if dx % 2 == 1 or (j, dx) == (far, 0):
+                odd = [a + b for a, b in zip(odd, got)]
+        return total, even, odd
+
+    steps = [[(1, 3), (1, 2)], [(0, 3), (0, 2)], [(1, 1), (1, 0)], [(0, 1), (0, 0)]]
     for h in range(PARTS - 1):
         lse_finish(h)
         for step in steps:
@@ -332,33 +362,28 @@
     to_sibling(3)
     to_sibling(2)
     second_pass(PARTS - 1, steps[1])
+    second_pass(PARTS - 1, steps[2])
     to_sibling(1)
     to_sibling(0)
-    second_pass(PARTS - 1, steps[2])
+    total, *even = to_owner(far)
+    to_owner(2)
     second_pass(PARTS - 1, steps[3])
-    to_owner(3)
-    to_owner(2)
     to_owner(1)
-    total, cnt, sq = to_owner(0)
-
-    tiles = [None, None]
-    for dx, j in sorted(others, key=lambda o: -o[1]):
-        arrived(r_in.at[j, dx], r_recv.at[j, dx])
-        total = total + r_in[j, dx, 0:OWN, :].astype(F32)
-        tile = r_in[j, dx, OWN:BLOCK, :].astype(F32)
-        tiles[dx % 2] = tile if tiles[dx % 2] is None else tiles[dx % 2] + tile
+    own_total, *own_even = to_owner(0)
+    total, even, odd = add_packets(total, even, None, [(far, dx) for dx in range(1, XS)])
+    lane = lax.broadcasted_iota(jnp.int32, (1, WIDTH), 1)
+    packet(far, 0, total, pack_stats(*[jnp.where(lane < OWN, a, b) for a, b in zip(even, odd)]))
+    send_packet(far, 0, 0, owner(0, far))
+    slots = [(j, dx) for j in range(far) for dx in range(XS) if (j, dx) != (0, 0)]
+    total, even, odd = add_packets(own_total, own_even, None, slots + [(far, 0)])
+
     is_cnt = (row < 3) & (col < WIDTH)
     is_sq = (row >= 3) & (row < 6) & (col >= WIDTH)
     columns = jnp.where(is_cnt | is_sq, 1.0, 0.0).astype(BF16)
     stats = 0.0
-    for odd in (0, 1):
-        t = tiles[odd]
-        c = t[0:1, :] + t[1:2, :] + t[2:3, :]
-        s = t[3:4, :] + t[4:5, :] + t[5:6, :]
-        if not odd:
-            c, s = c + cnt, s + sq
-        wide = spread_rows(pack_stats(c, s), columns)
-        stats = stats + wide[odd * OWN : (odd + 1) * OWN, :]
+    for i, rows in enumerate((even, odd)):
+        wide = spread_rows(pack_stats(*rows), columns)
+        stats = stats + wide[i * OWN : (i + 1) * OWN, :]
 
     counts = stats[:, 0:WIDTH]
     squares = -2.0 * stats[:, WIDTH:]

time: 48.2 us -> 45.4 us (0.942)
  Pallas kernels: 47.4 us -> 44.6 us
    pallas_call x1, Pallas kernels: 46 us -> 43.2 us  [per_device(): pl.pallas_call(functools.partial(body, comps, npoints, npoints * lax.axis...]
where the time goes in v3:
time: 45.4 us; the launch traced here: 45.2 us
  Pallas kernels  44.6 us (98%)
  between operations  0.64 us (1%)
    pallas_call x1, Pallas kernels, per_device(): pl.pallas_call(functools.partial(body, comps, npoints, npoints * lax.axis...  43.2 us
    pallas_call x1, Pallas kernels, per_device(): pl.pallas_call(finish, out_shape=[shape((own, WIDTH), BF16), shape((1, ow...  1.37 us

profile of v3, /device:TPU:1, one launch (start us, length us, event | category | flops | bytes accessed | tf_op | source)
XLA Modules:
  0.0 45.2 jit_solution(797912170878302187)
XLA Ops:
  0.6 43.2 %em_step.1 = (bf16[64,128]{1,0:T(8,128)(2,1)}, f32[1,64]{1,0:T(1,128)}, f32[1,64]{1,0:T(1,128)}, f32[1,4096]{1,0:T(1,128)}) custom-call(bf16[4096,128]{1,0:T(8,128)(2,1)} %points_hbm.1, bf16[64,128]{1,0:T(8,128)(2,1)} %means_hbm.1, f32[1,64]{1,0:T(1,128)} %bitcast.5, f32[1,64]{1,0:T(1,128)} %bitcast.6), custom_call_target="tpu_custom_call" | custom-call | tf_op jit(solution)/shard_map/em_step/pallas_call | solution.py:421
  43.9 1.4 %results.1 = (bf16[64,128]{1,0:T(8,128)(2,1)}, f32[1,64]{1,0:T(1,128)}, f32[1,64]{1,0:T(1,128)}, f32[1,4096]{1,0:T(1,128)}) custom-call(bf16[64,128]{1,0:T(8,128)(2,1)} %get-tuple-element.12.refs_0_, f32[1,64]{1,0:T(1,128)} %get-tuple-element.13.refs_1_, f32[1,64]{1,0:T(1,128)} %get-tuple-element.14.refs_2_, f32[1,4096]{1,0:T(1,128)} %get-tuple-element.15.refs_3_), custom_call_target="tpu_custom_call" | custom-call | tf_op jit(solution)/shard_map/results/pallas_call | solution.py:467

commit v4 on v3

--- a/solution.py
+++ b/solution.py
@@ -22,16 +22,19 @@
 WIDTH = 128
 OWN = 64
 BLOCK = 80
-CHUNK = 512
 TILE = 512
-PARTS = 2
 
 BASE = {
     (0, 0): 0, (1, 0): 4,
-    (0, 1): 8, (0, 2): 12,
-    (1, 1): 16, (1, 2): 20,
-    (0, 3): 24, (1, 3): 28,
+    (0, 1): 8, (1, 1): 12,
+    (0, 2): 16, (0, 3): 20,
+    (1, 2): 24, (1, 3): 28,
 }
+CHUNKS = [(1, 2, 3, 5, 6, 7), tuple(range(8, 16)), tuple(range(16, 24)), tuple(range(24, 32)), (0, 4)]
+BOUNDS = (0, 4, 8)
+PARTS = len(BOUNDS) - 1
+NEAR = (0, 1)
+FAR = (3, 2)
 GROUP = XS * OWN
 
 
@@ -64,19 +67,20 @@
 ):
     dp = lax.axis_index("dp")
     cp = lax.axis_index("comp")
-    core = dp % CORES
-    zh = (dp // CORES) % ZS
-    xx = dp // (CORES * ZS)
-    zl = cp % 2
-    yy = cp // 2
+    core = lax.rem(dp, CORES)
+    zh = lax.rem(lax.div(dp, CORES), ZS)
+    xx = lax.div(dp, CORES * ZS)
+    zl = lax.rem(cp, 2)
+    yy = lax.div(cp, 2)
     zz = zh * 2 + zl
     sign = 1 - 2 * zl
 
     def device(dx, dz, dc=0):
-        z = (zz + dz + Z) % Z
+        z = lax.rem(zz + dz + Z, Z)
+        half = lax.div(z, 2)
         return {
-            "dp": ((xx + dx) % XS) * (ZS * CORES) + (z // 2) * CORES + (core + dc) % CORES,
-            "comp": yy * 2 + z % 2,
+            "dp": lax.rem(xx + dx, XS) * (ZS * CORES) + half * CORES + lax.rem(core + dc, CORES),
+            "comp": yy * 2 + z - 2 * half,
         }
 
     def owner(dx, j, dc=0):
@@ -86,16 +90,13 @@
         return device(XS - dx, sign * j if j % 2 == 0 else -sign * j, dc)
 
     sibling = {"dp": dp + 1 - 2 * core}
-    c_peer = {d: {"comp": (cp + d) % comps} for d in range(1, comps)}
-    others = [(dx, j) for j in range(DEPTH - 1) for dx in range(XS) if (dx, j) != (0, 0)]
-    far = DEPTH - 1
-    others.append((0, far))
-
+    c_peer = {d: {"comp": lax.rem(cp + d, comps)} for d in range(1, comps)}
     barrier = pltpu.get_barrier_semaphore()
-    everyone = [sibling, *c_peer.values()]
-    everyone += [owner(dx, j) for dx, j in others]
-    everyone += [user(dx, 2) for dx in range(XS)]
-    everyone += [owner(dx, 0, 1) for dx in range(1, XS)]
+    everyone = [owner(0, 3), *(c_peer[d] for d in (5, 4, 3, 2, 6, 7, 1))]
+    for dx in (2, 1, 3, 0):
+        everyone += [owner(dx, 1, dc) for dc in range(CORES)]
+    everyone += [owner(0, 2), user(0, 2)]
+    everyone += [owner(dx, 0, dc) for dx in (2, 1, 3) for dc in range(CORES)] + [sibling]
     for peer in everyone:
         pl.semaphore_signal(barrier, inc=1, device_id=peer, device_id_type=MESH)
     fetches = [
@@ -154,7 +155,7 @@
 
     fetches[3].wait()
     steps = npoints // WIDTH // 4
-    lax.fori_loop(0, steps // 2, prepare, 0)
+    lax.fori_loop(0, steps // 4, prepare, 0)
 
     pl.semaphore_wait(barrier, len(everyone))
 
@@ -185,98 +186,108 @@
         arrived(blocks.at[pl.ds(slot, n)], g_recv.at[slot])
 
     gather_send(0, BASE[1, 0], 1, sibling)
-    for dx in (2, 1, 3):
-        gather_send(0, BASE[0, 0] + dx, 1, user(dx, 0))
-        gather_send(0, BASE[1, 0] + dx, 1, user(dx, 0, 1))
-    gather_send(0, BASE[0, far], 1, user(0, far))
-    for j in (1, 2):
+    for j in FAR:
+        gather_send(0, BASE[0, j], 1, user(0, j))
+    for j in NEAR:
         for dx in (2, 1, 3, 0):
-            gather_send(0, BASE[0, j] + dx, 1, user(dx, j))
-
-    lax.fori_loop(steps // 2, steps, prepare, 0)
-
-    row = lax.broadcasted_iota(jnp.int32, (16, 2 * WIDTH), 0)
-    col = lax.broadcasted_iota(jnp.int32, (16, 2 * WIDTH), 1)
+            if (dx, j) != (0, 0):
+                for dc in range(CORES):
+                    gather_send(0, BASE[dc, j] + dx, 1, user(dx, j, dc))
+    lax.fori_loop(steps // 4, steps, prepare, 0)
+
+    row = lax.broadcasted_iota(jnp.int32, (WIDTH, 2 * WIDTH), 0) % 16
+    col = lax.broadcasted_iota(jnp.int32, (WIDTH, 2 * WIDTH), 1)
     put = ((row < 3) & (col == row)) | ((row == 6) & (col >= 3) & (col < 6))
     put = put | ((row >= 3) & (row < 6) & (col >= WIDTH))
     table = jnp.where(put, 1.0, 0.0).astype(BF16)
 
-    def expand(first, n):
-        for s in range(first, first + n):
+    def expand(c):
+        n = len(CHUNKS[c])
+        rows = [blocks[s, OWN:BLOCK, :] for s in CHUNKS[c]]
+        turned = jnp.concatenate(rows, axis=0).astype(F32).T[0:OWN, :]
+        home = lax.broadcasted_iota(jnp.int32, (OWN, 16 * n), 1) // 16
+        mine = [jnp.where(home == i, turned, 0.0).astype(BF16) for i in range(n)]
+        wide = jnp.dot(
+            jnp.concatenate(mine, axis=0), table[0 : 16 * n, :], preferred_element_type=F32
+        )
+        for i, s in enumerate(CHUNKS[c]):
             at = slice(s * OWN, (s + 1) * OWN)
-            wide = spread_rows(blocks[s, OWN:BLOCK, :], table)[0:OWN, :]
             centres[at, 0:WIDTH] = blocks[s, 0:OWN, :]
-            centres[at, WIDTH : 2 * WIDTH] = wide[:, 0:WIDTH].astype(BF16)
-            scale[at, :] = wide[:, WIDTH : 2 * WIDTH]
+            centres[at, WIDTH : 2 * WIDTH] = wide[i * OWN : (i + 1) * OWN, 0:WIDTH].astype(BF16)
+            scale[at, :] = wide[i * OWN : (i + 1) * OWN, WIDTH : 2 * WIDTH]
 
     def first_pass(c, first, last):
-        at = slice(c * CHUNK, (c + 1) * CHUNK)
+        rows = [slice(b * OWN, (b + 1) * OWN) for b in CHUNKS[c]]
+        whole = jnp.concatenate([centres[at, :] for at in rows], axis=0)
+        wide = jnp.concatenate([scale[at, :] for at in rows], axis=0)
+        wide = jnp.concatenate([wide] * (TILE // WIDTH), axis=1)
         for t in range(first // TILE, last // TILE):
             ns = slice(t * TILE, (t + 1) * TILE)
-            y = jnp.dot(centres[at, :], pts_t[:, ns], preferred_element_type=F32)
-            y = y * jnp.concatenate([scale[at, :]] * (TILE // WIDTH), axis=1)
+            y = jnp.dot(whole, pts_t[:, ns], preferred_element_type=F32) * wide
             top = jnp.max(y, axis=0, keepdims=True)
             p = jnp.exp2(y - top)
-            prob[at, ns] = p
+            for i, at in enumerate(rows):
+                prob[at, ns] = p[i * OWN : (i + 1) * OWN, :]
             peak[c : c + 1, ns] = top
             mass[c : c + 1, ns] = jnp.sum(p, axis=0, keepdims=True)
 
-    chunks = 4
-    part = npoints // PARTS
-    parts = [slice(h * part, (h + 1) * part) for h in range(PARTS)]
+    chunks = len(CHUNKS)
+    bounds = [npoints * i // 8 for i in BOUNDS]
+    parts = [slice(a, b) for a, b in zip(bounds, bounds[1:])]
 
     def lse_send(h):
         ns = parts[h]
         top = jnp.max(peak[0:chunks, ns], axis=0, keepdims=True)
         total = jnp.sum(mass[0:chunks, ns] * jnp.exp2(peak[0:chunks, ns] - top), axis=0, keepdims=True)
-        lse[h, 0] = top + jnp.log(total) * LOG2E
+        n = ns.stop - ns.start
+        lse[h, 0, :, 0:n] = top + jnp.log(total) * LOG2E
         for d in range(1, comps):
             remote(
-                lse.at[h, 0], lse.at[h, comps - d],
+                lse.at[h, 0, :, pl.ds(0, n)], lse.at[h, comps - d, :, pl.ds(0, n)],
                 l_send.at[h, d], l_recv.at[h, comps - d], c_peer[d],
             )
 
     def lse_finish(h):
         ns = parts[h]
+        n = ns.stop - ns.start
         for d in range(1, comps):
-            arrived(lse.at[h, d], l_recv.at[h, d])
-        top = lse[h, 0]
-        for d in range(1, comps):
-            top = jnp.maximum(top, lse[h, d])
-        total = jnp.exp2(lse[h, 0] - top)
-        for d in range(1, comps):
-            total = total + jnp.exp2(lse[h, d] - top)
+            arrived(lse.at[h, d, :, pl.ds(0, n)], l_recv.at[h, d])
+        got = [lse[h, d, :, 0:n] for d in range(comps)]
+        top = functools.reduce(jnp.maximum, got)
+        total = sum(jnp.exp2(g - top) for g in got)
         lik = top + jnp.log(total) * LOG2E
         out_lik[:, ns] = lik * LN2
         for c in range(chunks):
             peak[c : c + 1, ns] = jnp.exp2(peak[c : c + 1, ns] - lik)
 
-    for dx in range(XS):
-        if dx:
-            gather_wait(BASE[0, 0] + dx, 1)
-        gather_wait(BASE[1, 0] + dx, 1)
-    expand(0, 8)
+    gather_wait(BASE[1, 0], 1)
+    expand(4)
+    first_pass(4, 0, npoints)
+    for dc in range(CORES):
+        for dx in range(1, XS):
+            gather_wait(BASE[dc, 0] + dx, 1)
+    expand(0)
+    for j in FAR:
+        gather_wait(BASE[0, j], 1)
+        for d in (2, 1, 3):
+            gather_send(BASE[0, j], BASE[0, j] + XS - d, 1, device(d, 0))
     first_pass(0, 0, npoints)
-    gather_wait(BASE[0, far], 1)
-    for d in (2, 1, 3):
-        gather_send(BASE[0, far], BASE[0, far] + XS - d, 1, device(d, 0))
-    for j in (1, 2):
+    for dc in range(CORES):
         for dx in range(XS):
+            gather_wait(BASE[dc, 1] + dx, 1)
+    expand(1)
+    first_pass(1, 0, npoints)
+    for j in FAR:
+        for dx in range(1, XS):
             gather_wait(BASE[0, j] + dx, 1)
         gather_send(BASE[0, j], BASE[1, j], XS, sibling)
-    expand(8, 8)
-    first_pass(1, 0, npoints)
-    for dx in range(1, XS):
-        gather_wait(BASE[0, far] + dx, 1)
-    gather_send(BASE[0, far], BASE[1, far], XS, sibling)
-    gather_wait(BASE[1, 1], XS)
-    gather_wait(BASE[1, 2], XS)
-    expand(16, 12)
+    expand(2)
     for h in range(PARTS):
         first_pass(2, parts[h].start, parts[h].stop)
         if h == 0:
-            gather_wait(BASE[1, far], XS)
-            expand(28, 4)
+            for j in FAR:
+                gather_wait(BASE[1, j], XS)
+            expand(3)
         first_pass(3, parts[h].start, parts[h].stop)
         lse_send(h)
 
@@ -284,9 +295,10 @@
         ns = parts[h]
         p = []
         for g in groups:
-            first = BASE[g] * OWN
-            c = first // CHUNK
-            p.append((prob[first : first + GROUP, ns] * peak[c : c + 1, ns]).astype(BF16))
+            for b in range(BASE[g], BASE[g] + XS):
+                c = [b in blocks_of for blocks_of in CHUNKS].index(True)
+                at = slice(b * OWN, (b + 1) * OWN)
+                p.append((prob[at, ns] * peak[c : c + 1, ns]).astype(BF16))
         acc = jnp.dot(jnp.concatenate(p, axis=0), pts[ns, :], preferred_element_type=F32)
         for i, g in enumerate(groups):
             at = slice(BASE[g] * OWN, BASE[g] * OWN + GROUP)
@@ -326,11 +338,11 @@
         tot, cnt, sq = chip_sum(j)
         tile = pack_stats(cnt, sq)
         for dx in (2, 1, 3, 0):
-            if dx == 0 and j in (0, far):
+            if dx == 0 and (j == 0 or j in FAR):
                 continue
             lanes = slice((dx // 2) * WIDTH, (dx // 2 + 1) * WIDTH)
             packet(j, dx, tot[dx * OWN : (dx + 1) * OWN, :], tile[:, lanes])
-            if j == far:
+            if j in FAR:
                 send_packet(j, dx, XS - dx, device(dx, 0))
             else:
                 send_packet(j, dx, dx, owner(dx, j))
@@ -348,7 +360,7 @@
             got = rows_of(r_in[j, dx, OWN:BLOCK, :])
             if dx % 2 == 0:
                 even = [a + b for a, b in zip(even, got)]
-            if dx % 2 == 1 or (j, dx) == (far, 0):
+            if dx % 2 == 1 or (dx == 0 and j in FAR):
                 odd = [a + b for a, b in zip(odd, got)]
         return total, even, odd
 
@@ -362,21 +374,22 @@
     to_sibling(3)
     to_sibling(2)
     second_pass(PARTS - 1, steps[1])
+    partial = {j: to_owner(j) for j in FAR}
     second_pass(PARTS - 1, steps[2])
     to_sibling(1)
     to_sibling(0)
-    total, *even = to_owner(far)
-    to_owner(2)
     second_pass(PARTS - 1, steps[3])
     to_owner(1)
     own_total, *own_even = to_owner(0)
-    total, even, odd = add_packets(total, even, None, [(far, dx) for dx in range(1, XS)])
     lane = lax.broadcasted_iota(jnp.int32, (1, WIDTH), 1)
-    packet(far, 0, total, pack_stats(*[jnp.where(lane < OWN, a, b) for a, b in zip(even, odd)]))
-    send_packet(far, 0, 0, owner(0, far))
-    slots = [(j, dx) for j in range(far) for dx in range(XS) if (j, dx) != (0, 0)]
-    total, even, odd = add_packets(own_total, own_even, None, slots + [(far, 0)])
-
+    for j in FAR:
+        total, *even = partial[j]
+        total, even, odd = add_packets(total, even, None, [(j, dx) for dx in range(1, XS)])
+        packet(j, 0, total, pack_stats(*[jnp.where(lane < OWN, a, b) for a, b in zip(even, odd)]))
+        send_packet(j, 0, 0, owner(0, j))
+    slots = [(j, dx) for j in NEAR for dx in range(XS) if (dx, j) != (0, 0)]
+    total, even, odd = add_packets(own_total, own_even, None, slots + [(j, 0) for j in FAR])
+    row, col = row[0:16, :], col[0:16, :]
     is_cnt = (row < 3) & (col < WIDTH)
     is_sq = (row >= 3) & (row < 6) & (col >= WIDTH)
     columns = jnp.where(is_cnt | is_sq, 1.0, 0.0).astype(BF16)
@@ -441,7 +454,7 @@
             pltpu.VMEM((group, npoints), F32),
             pltpu.VMEM((8, npoints), F32),
             pltpu.VMEM((8, npoints), F32),
-            pltpu.VMEM((PARTS, comps, 1, npoints // PARTS), F32),
+            pltpu.VMEM((PARTS, comps, 1, npoints // 2), F32),
             pltpu.VMEM((group, 2 * WIDTH), F32),
             pltpu.VMEM((DEPTH, GROUP, WIDTH), F32),
             pltpu.VMEM((DEPTH, GROUP, WIDTH), F32),

time: 45.4 us -> 45.2 us (level)
  no operation moved by 1% of the time
where the time goes in v4:
time: 45.2 us; the launch traced here: 45 us
  Pallas kernels  44.4 us (98%)
  between operations  0.64 us (1%)
    pallas_call x1, Pallas kernels, per_device(): pl.pallas_call(functools.partial(body, comps, npoints, npoints * lax.axis...  43 us
    pallas_call x1, Pallas kernels, per_device(): pl.pallas_call(finish, out_shape=[shape((own, WIDTH), BF16), shape((1, ow...  1.37 us

profile of v4, /device:TPU:1, one launch (start us, length us, event | category | flops | bytes accessed | tf_op | source)
XLA Modules:
  0.0 45.0 jit_solution(18439373719710099904)
XLA Ops:
  0.6 43.0 %em_step.1 = (bf16[64,128]{1,0:T(8,128)(2,1)}, f32[1,64]{1,0:T(1,128)}, f32[1,64]{1,0:T(1,128)}, f32[1,4096]{1,0:T(1,128)}) custom-call(bf16[4096,128]{1,0:T(8,128)(2,1)} %points_hbm.1, bf16[64,128]{1,0:T(8,128)(2,1)} %means_hbm.1, f32[1,64]{1,0:T(1,128)} %bitcast.5, f32[1,64]{1,0:T(1,128)} %bitcast.6), custom_call_target="tpu_custom_call" | custom-call | tf_op jit(solution)/shard_map/em_step/pallas_call | solution.py:434
  43.7 1.4 %results.1 = (bf16[64,128]{1,0:T(8,128)(2,1)}, f32[1,64]{1,0:T(1,128)}, f32[1,64]{1,0:T(1,128)}, f32[1,4096]{1,0:T(1,128)}) custom-call(bf16[64,128]{1,0:T(8,128)(2,1)} %get-tuple-element.12.refs_0_, f32[1,64]{1,0:T(1,128)} %get-tuple-element.13.refs_1_, f32[1,64]{1,0:T(1,128)} %get-tuple-element.14.refs_2_, f32[1,4096]{1,0:T(1,128)} %get-tuple-element.15.refs_3_), custom_call_target="tpu_custom_call" | custom-call | tf_op jit(solution)/shard_map/results/pallas_call | solution.py:480

commit v5 on v4

--- a/solution.py
+++ b/solution.py
@@ -370,9 +370,9 @@
         for step in steps:
             second_pass(h, step)
     lse_finish(PARTS - 1)
-    second_pass(PARTS - 1, steps[0])
-    to_sibling(3)
-    to_sibling(2)
+    for j in FAR:
+        second_pass(PARTS - 1, [(1, j)])
+        to_sibling(j)
     second_pass(PARTS - 1, steps[1])
     partial = {j: to_owner(j) for j in FAR}
     second_pass(PARTS - 1, steps[2])

time: 45.2 us -> 45.1 us (level)
  no operation moved by 1% of the time
where the time goes in v5:
time: 45.1 us; the launch traced here: 45 us
  Pallas kernels  44.3 us (98%)
  between operations  0.64 us (1%)
    pallas_call x1, Pallas kernels, per_device(): pl.pallas_call(functools.partial(body, comps, npoints, npoints * lax.axis...  43 us
    pallas_call x1, Pallas kernels, per_device(): pl.pallas_call(finish, out_shape=[shape((own, WIDTH), BF16), shape((1, ow...  1.37 us

profile of v5, /device:TPU:1, one launch (start us, length us, event | category | flops | bytes accessed | tf_op | source)
XLA Modules:
  0.0 45.0 jit_solution(7502623492100943995)
XLA Ops:
  0.6 43.0 %em_step.1 = (bf16[64,128]{1,0:T(8,128)(2,1)}, f32[1,64]{1,0:T(1,128)}, f32[1,64]{1,0:T(1,128)}, f32[1,4096]{1,0:T(1,128)}) custom-call(bf16[4096,128]{1,0:T(8,128)(2,1)} %points_hbm.1, bf16[64,128]{1,0:T(8,128)(2,1)} %means_hbm.1, f32[1,64]{1,0:T(1,128)} %bitcast.5, f32[1,64]{1,0:T(1,128)} %bitcast.6), custom_call_target="tpu_custom_call" | custom-call | tf_op jit(solution)/shard_map/em_step/pallas_call | solution.py:434
  43.6 1.4 %results.1 = (bf16[64,128]{1,0:T(8,128)(2,1)}, f32[1,64]{1,0:T(1,128)}, f32[1,64]{1,0:T(1,128)}, f32[1,4096]{1,0:T(1,128)}) custom-call(bf16[64,128]{1,0:T(8,128)(2,1)} %get-tuple-element.12.refs_0_, f32[1,64]{1,0:T(1,128)} %get-tuple-element.13.refs_1_, f32[1,64]{1,0:T(1,128)} %get-tuple-element.14.refs_2_, f32[1,4096]{1,0:T(1,128)} %get-tuple-element.15.refs_3_), custom_call_target="tpu_custom_call" | custom-call | tf_op jit(solution)/shard_map/results/pallas_call | solution.py:480
